TPU v7x, 256 devices: a whole 4x4x8 slice. The times are simulated.
256 devices in a mesh: row: 32 (over z, x_lo, core), col: 8 (over x_hi, y).
Axes of the slice: x: 4 (x_hi: 2, x_lo: 2; x = x_hi * 2 + x_lo), y: 4, z: 8, core: 2. Of those that a mesh axis runs over, the one named last changes fastest.
Arguments:
- queries: bfloat16 [1, 128, 128, 1536], P(None, 'row', 'col'), may hold values from -180 to 180
- key_tokens: bfloat16 [1, 128, 128, 1536], P(None, 'row', 'col'), may hold values from -4 to 4
- values: bfloat16 [1, 128, 128, 1536], P(None, 'row', 'col'), may hold values from -6 to 6
- position_bias: float32 [24, 49], replicated, may hold values from -4 to 4
- out_weight: bfloat16 [1536, 1536], P('col', 'row'), may hold values from -0.15625 to 0.15625
Outputs:
- projected: bfloat16 [1, 128, 128, 1536], P(None, 'row', 'col')
All inputs are finite; a program needn't handle non-finite values.
Results may differ from a plain program's by a relative error of at most 0.0057.
Values may be sent and summed in bfloat16 or wider, within the bound.
No kernel may reach another device: no remote copies, remote signals or barrier semaphores. Data moves between devices by JAX's collectives and lax.ppermute only.
A program may use at most 64 MiB of HBM per device.

v0:
```python
import math
import jax
import jax.numpy as jnp
from jax import lax
from jax.sharding import PartitionSpec as P


def extended_2(block, sides, width):
    for axis, dim in sides:
        count = lax.axis_size(axis)
        forward = [(i, i + 1) for i in range(count - 1)]
        backward = [(target, source) for source, target in forward]
        low = lax.ppermute(
            lax.slice_in_dim(block, block.shape[dim] - width, None, axis=dim), axis, forward
        )
        high = lax.ppermute(lax.slice_in_dim(block, 0, width, axis=dim), axis, backward)
        block = jnp.concatenate([low, block, high], axis=dim)
    return block


def shards(queries, key_tokens, values, position_bias, out_weight):
    images = queries.shape[0]
    band_rows = queries.shape[1]
    strip_cols = queries.shape[2]
    model_width = queries.shape[3]
    head_count = position_bias.shape[0]
    head_size = model_width // head_count
    height = band_rows * lax.axis_size("row")
    breadth = strip_cols * lax.axis_size("col")
    stacked = jnp.stack([key_tokens, values], 0)
    extended = extended_2(stacked, (("row", 2), ("col", 3)), 3)
    key_ext = extended[0]
    value_ext = extended[1]
    query_heads = queries.reshape(images, band_rows, strip_cols, head_count, head_size)
    global_rows = lax.axis_index("row") * band_rows + jnp.arange(band_rows)
    global_cols = lax.axis_index("col") * strip_cols + jnp.arange(strip_cols)
    offsets = jnp.arange(7) - 3
    rows_inside = (global_rows[None, :] + offsets[:, None] >= 0) & (
        global_rows[None, :] + offsets[:, None] < height
    )
    cols_inside = (global_cols[None, :] + offsets[:, None] >= 0) & (
        global_cols[None, :] + offsets[:, None] < breadth
    )
    inside = (rows_inside[:, None, :, None] & cols_inside[None, :, None, :]).reshape(
        49, 1, band_rows, strip_cols, 1
    )
    score_scale = 1.0 / math.sqrt(head_size)
    row_steps = jnp.arange(7, dtype=jnp.int32)

    def score_step(carry, row_off):
        band_keys = lax.dynamic_slice_in_dim(key_ext, row_off, band_rows, 1)
        row_scores = []
        for col_off in range(7):
            window = band_keys[:, :, col_off : col_off + strip_cols].reshape(
                images, band_rows, strip_cols, head_count, head_size
            )
            row_scores.append(
                jnp.einsum(
                    "ibshd,ibshd->ibsh", query_heads, window, preferred_element_type=jnp.float32
                )
            )
        return (carry, jnp.stack(row_scores, 0))

    unused, score_grid = lax.scan(score_step, jnp.zeros((), jnp.float32), row_steps)
    scores = score_grid.reshape(49, images, band_rows, strip_cols, head_count) * score_scale
    scores = scores + jnp.transpose(position_bias)[:, None, None, None, :]
    scores = jnp.where(inside, scores, -jnp.inf)
    attention = jax.nn.softmax(scores, axis=0).astype(jnp.bfloat16)
    attention_grid = attention.reshape(7, 7, images, band_rows, strip_cols, head_count)

    def value_step(summed, items):
        row_off, weights = items
        band_values = lax.dynamic_slice_in_dim(value_ext, row_off, band_rows, 1)
        row_total = None
        for col_off in range(7):
            window = band_values[:, :, col_off : col_off + strip_cols].reshape(
                images, band_rows, strip_cols, head_count, head_size
            )
            term = weights[col_off].astype(jnp.float32)[..., None] * window.astype(jnp.float32)
            row_total = term if row_total is None else row_total + term
        return (summed + row_total, None)

    initial_sum = jnp.zeros((images, band_rows, strip_cols, head_count, head_size), jnp.float32)
    summed, unused_out = lax.scan(value_step, initial_sum, (row_steps, attention_grid))
    mixed_heads = summed.astype(jnp.bfloat16).reshape(images * band_rows * strip_cols, model_width)
    tall_weight = lax.all_gather(out_weight, "col", axis=0, tiled=True)
    result = jnp.dot(
        mixed_heads,
        lax.all_gather(tall_weight, "row", axis=1, tiled=True),
        preferred_element_type=jnp.float32,
    )
    return result.astype(jnp.bfloat16).reshape(images, band_rows, strip_cols, model_width)


def solution(mesh):
    in_specs = (
        P(None, "row", "col", None),
        P(None, "row", "col", None),
        P(None, "row", "col", None),
        P(),
        P("col", "row"),
    )
    out_specs = P(None, "row", "col", None)
    return jax.shard_map(shards, mesh=mesh, in_specs=in_specs, out_specs=out_specs, check_vma=False)
```

profile of v0, /device:TPU:248, one launch (start us, length us, event | category | flops | bytes accessed | tf_op | source)
XLA Modules:
  0.0 312.8 jit_solution(8154622619189542940)
XLA Ops:
  9.8 4.5 %collective-permute-start.1 = (bf16[2,1,3,16,1536]{4,3,2,1,0:T(8,128)(2,1)S(1)}, bf16[2,1,3,16,1536]{4,3,2,1,0:T(8,128)(2,1)S(1)}, u32[]{:S(2)}, u32[]{:S(2)}) collective-permute-start(bf16[2,1,3,16,1536]{4,3,2,1,0:T(8,128)(2,1)S(1)} %get-tuple-element.132), channel_id=1, source_target_pairs={{8,0},{16,8},{24,16},{32,24},{40,32},{48,40},{56,48},{64,56},{72,6... | collective-permute-start | bytes 884744 | tf_op jit(solution)/shard_map/ppermute | solution.py:16
  14.3 34.5 %all-gather = bf16[8,192,48]{1,2,0:T(8,128)(2,1)S(1)} all-gather(bf16[1,192,48]{1,2,0:T(8,128)(2,1)} %bitcast.136), channel_id=1, replica_groups=mesh['row'=32,'col'=8] {'col'}, dimensions={0}, use_global_device_ids=true | all-gather | bytes 165888 | tf_op jit(solution)/shard_map/all_gather | solution.py:86
  51.3 4.6 %collective-permute-start.2 = (bf16[2,1,10,3,1536]{4,3,2,1,0:T(4,128)(2,1)S(1)}, bf16[2,1,10,3,1536]{4,3,2,1,0:T(4,128)(2,1)S(1)}, u32[]{:S(2)}, u32[]{:S(2)}) collective-permute-start(bf16[2,1,10,3,1536]{4,3,2,1,0:T(4,128)(2,1)S(1)} %get-tuple-element.129), channel_id=1, source_target_pairs={{0,1},{1,2},{2,3},{3,4},{4,5},{5,6},{6,7},{8,9},{9,10},{10,11},{11... | collective-permute-start | bytes 552968 | tf_op jit(solution)/shard_map/ppermute | solution.py:13
  59.7 9.8 %collective-permute-done.3 = bf16[2,1,10,3,1536]{4,3,2,1,0:T(4,128)(2,1)S(1)} collective-permute-done((bf16[2,1,10,3,1536]{4,3,2,1,0:T(4,128)(2,1)S(1)}, bf16[2,1,10,3,1536]{4,3,2,1,0:T(4,128)(2,1)S(1)}, u32[]{:S(2)}, u32[]{:S(2)}) %collective-permute-start.3) | collective-permute-done | bytes 184352 | tf_op jit(solution)/shard_map/ppermute | solution.py:16
  70.3 93.0 %while.21 = (s32[]{:T(128)}, f32[7,7,1,4,16,24]{5,4,3,2,1,0:T(8,128)}, s32[7]{0:T(128)S(1)}, bf16[1,10,22,1536]{3,2,1,0:T(8,128)(2,1)S(1)}, bf16[1,4,16,24,64]{4...) while((s32[]{:T(128)}, ...), condition=%wide.region_1.2_spmd, body=%wide.region_0.1_spmd.sunk | while | flops 2151947 | bytes 7826199 | solution.py:64
  80.0 2.7 fusion.23
  93.3 2.7 fusion.23
  106.6 2.8 fusion.23
  119.9 2.7 fusion.23
  133.2 2.7 fusion.23
  146.5 2.7 fusion.23
  159.8 2.7 fusion.23
  166.8 2.6 divide_convert_fusion
  169.4 130.5 %while.22 = (s32[]{:T(128)}, f32[1,4,16,24,64]{4,3,2,1,0:T(8,128)}, bf16[7,7,1,4,16,24]{5,4,3,2,1,0:T(8,128)(2,1)}, s32[7]{0:T(128)S(1)}, bf16[1,10,22,1536]{3,2...) while((s32[]{:T(128)}, f32[1,4,16,24,64]{4,3,2,1,0:T(8,128)}, ...), condition=%wide.region_5.6_spmd.clone, body=%wide.region_4.5_spmd.clone.sunk | while | flops 2173452 | bytes 13280573 | solution.py:84
  179.2 2.1 reshape.518
  183.3 4.7 %select_add_fusion.2 = f32[1,4,16,24,64]{4,3,2,1,0:T(8,128)} fusion(f32[1,4,16,24,64]{4,3,2,1,0:T(8,128)} %get-tuple-element.308, f32[1,4,16,24,64]{4,3,2,1,0:T(8,128)S(1)} %reshape.513, f32[1,4,16,24,64]{4,3,2,1,0:T(8,128)S(1)} %reshape.514, f32[1,4,16,24,64]{4,3,2,1,0:T(8,128)S(1)} %reshape.515, f32[1,4,16,24,64]{4,3,2,1,0:T(8,128)} %reshape.516, ...), kind=kLoop, calls=%fused_computation.clone.1 | loop fusion | flops 1474560 | bytes 3581953 | tf_op jit(solution)/shard_map/while/body/eval_jaxpr/add | solution.py:81
  197.7 2.1 reshape.518
  201.8 4.8 %select_add_fusion.2 = f32[1,4,16,24,64]{4,3,2,1,0:T(8,128)} fusion(f32[1,4,16,24,64]{4,3,2,1,0:T(8,128)} %get-tuple-element.308, f32[1,4,16,24,64]{4,3,2,1,0:T(8,128)S(1)} %reshape.513, f32[1,4,16,24,64]{4,3,2,1,0:T(8,128)S(1)} %reshape.514, f32[1,4,16,24,64]{4,3,2,1,0:T(8,128)S(1)} %reshape.515, f32[1,4,16,24,64]{4,3,2,1,0:T(8,128)} %reshape.516, ...), kind=kLoop, calls=%fused_computation.clone.1 | loop fusion | flops 1474560 | bytes 3581953 | tf_op jit(solution)/shard_map/while/body/eval_jaxpr/add | solution.py:81
  220.5 4.8 %select_add_fusion.2 = f32[1,4,16,24,64]{4,3,2,1,0:T(8,128)} fusion(f32[1,4,16,24,64]{4,3,2,1,0:T(8,128)} %get-tuple-element.308, f32[1,4,16,24,64]{4,3,2,1,0:T(8,128)S(1)} %reshape.513, f32[1,4,16,24,64]{4,3,2,1,0:T(8,128)S(1)} %reshape.514, f32[1,4,16,24,64]{4,3,2,1,0:T(8,128)S(1)} %reshape.515, f32[1,4,16,24,64]{4,3,2,1,0:T(8,128)} %reshape.516, ...), kind=kLoop, calls=%fused_computation.clone.1 | loop fusion | flops 1474560 | bytes 3581953 | tf_op jit(solution)/shard_map/while/body/eval_jaxpr/add | solution.py:81
  239.1 4.8 %select_add_fusion.2 = f32[1,4,16,24,64]{4,3,2,1,0:T(8,128)} fusion(f32[1,4,16,24,64]{4,3,2,1,0:T(8,128)} %get-tuple-element.308, f32[1,4,16,24,64]{4,3,2,1,0:T(8,128)S(1)} %reshape.513, f32[1,4,16,24,64]{4,3,2,1,0:T(8,128)S(1)} %reshape.514, f32[1,4,16,24,64]{4,3,2,1,0:T(8,128)S(1)} %reshape.515, f32[1,4,16,24,64]{4,3,2,1,0:T(8,128)} %reshape.516, ...), kind=kLoop, calls=%fused_computation.clone.1 | loop fusion | flops 1474560 | bytes 3581953 | tf_op jit(solution)/shard_map/while/body/eval_jaxpr/add | solution.py:81
  257.8 4.8 %select_add_fusion.2 = f32[1,4,16,24,64]{4,3,2,1,0:T(8,128)} fusion(f32[1,4,16,24,64]{4,3,2,1,0:T(8,128)} %get-tuple-element.308, f32[1,4,16,24,64]{4,3,2,1,0:T(8,128)S(1)} %reshape.513, f32[1,4,16,24,64]{4,3,2,1,0:T(8,128)S(1)} %reshape.514, f32[1,4,16,24,64]{4,3,2,1,0:T(8,128)S(1)} %reshape.515, f32[1,4,16,24,64]{4,3,2,1,0:T(8,128)} %reshape.516, ...), kind=kLoop, calls=%fused_computation.clone.1 | loop fusion | flops 1474560 | bytes 3581953 | tf_op jit(solution)/shard_map/while/body/eval_jaxpr/add | solution.py:81
  276.4 4.8 %select_add_fusion.2 = f32[1,4,16,24,64]{4,3,2,1,0:T(8,128)} fusion(f32[1,4,16,24,64]{4,3,2,1,0:T(8,128)} %get-tuple-element.308, f32[1,4,16,24,64]{4,3,2,1,0:T(8,128)S(1)} %reshape.513, f32[1,4,16,24,64]{4,3,2,1,0:T(8,128)S(1)} %reshape.514, f32[1,4,16,24,64]{4,3,2,1,0:T(8,128)S(1)} %reshape.515, f32[1,4,16,24,64]{4,3,2,1,0:T(8,128)} %reshape.516, ...), kind=kLoop, calls=%fused_computation.clone.1 | loop fusion | flops 1474560 | bytes 3581953 | tf_op jit(solution)/shard_map/while/body/eval_jaxpr/add | solution.py:81
  295.1 4.8 %select_add_fusion.2 = f32[1,4,16,24,64]{4,3,2,1,0:T(8,128)} fusion(f32[1,4,16,24,64]{4,3,2,1,0:T(8,128)} %get-tuple-element.308, f32[1,4,16,24,64]{4,3,2,1,0:T(8,128)S(1)} %reshape.513, f32[1,4,16,24,64]{4,3,2,1,0:T(8,128)S(1)} %reshape.514, f32[1,4,16,24,64]{4,3,2,1,0:T(8,128)S(1)} %reshape.515, f32[1,4,16,24,64]{4,3,2,1,0:T(8,128)} %reshape.516, ...), kind=kLoop, calls=%fused_computation.clone.1 | loop fusion | flops 1474560 | bytes 3581953 | tf_op jit(solution)/shard_map/while/body/eval_jaxpr/add | solution.py:81
  301.4 4.5 %convolution_convert_fusion = bf16[64,1536]{1,0:T(8,128)(2,1)} fusion(bf16[64,1536]{1,0:T(8,128)(2,1)S(1)} %reshape.439, bf16[1536,1536]{0,1:T(8,128)(2,1)} %all-gather.3.cloned.1.call-done), kind=kOutput, calls=%fused_computation.51 | convolution fusion | flops 302088192 | bytes 5111808 | tf_op jit(solution)/shard_map/dot_general | solution.py:87
  (226 shorter events, 153.5 us)
Async XLA Ops:
  6.5 44.6 %copy-start = (bf16[1,4,16,1536]{3,2,1,0:T(8,128)(2,1)S(1)}, bf16[1,4,16,1536]{3,2,1,0:T(8,128)(2,1)}, u32[]{:S(2)}) copy-start(bf16[1,4,16,1536]{3,2,1,0:T(8,128)(2,1)} %param.10) | copy-start | bytes 589828
  6.5 44.6 %copy-start.1 = (bf16[1,4,16,1536]{3,2,1,0:T(8,128)(2,1)S(1)}, bf16[1,4,16,1536]{3,2,1,0:T(8,128)(2,1)}, u32[]{:S(2)}) copy-start(bf16[1,4,16,1536]{3,2,1,0:T(8,128)(2,1)} %param.11) | copy-start | bytes 589828
  6.5 43.3 %copy-start.2 = (bf16[1,4,16,1536]{3,2,1,0:T(8,128)(2,1)S(1)}, bf16[1,4,16,1536]{3,2,1,0:T(8,128)(2,1)}, u32[]{:S(2)}) copy-start(bf16[1,4,16,1536]{3,2,1,0:T(8,128)(2,1)} %param.9) | copy-start | bytes 589828
  6.5 44.3 %copy-start.3 = (f32[24,49]{1,0:T(8,128)S(1)}, f32[24,49]{1,0:T(8,128)}, u32[]{:S(2)}) copy-start(f32[24,49]{1,0:T(8,128)} %param.12) | copy-start | bytes 14116
  6.5 294.8 %all-gather.3.cloned.1.call-start = ((), (), s32[]{:S(2)}) async-start(), calls=%async_computation | async-start | bytes 4866048 | tf_op jit(solution)/shard_map/all_gather | solution.py:89
  7.8 43.2 %collective-permute-start = (bf16[2,1,3,16,1536]{4,3,2,1,0:T(8,128)(2,1)S(1)}, bf16[2,1,3,16,1536]{4,3,2,1,0:T(8,128)(2,1)S(1)}, u32[]{:S(2)}, u32[]{:S(2)}) collective-permute-start(bf16[2,1,3,16,1536]{4,3,2,1,0:T(8,128)(2,1)S(1)} %get-tuple-element.131), channel_id=1, source_target_pairs={{0,8},{8,16},{16,24},{24,32},{32,40},{40,48},{48,56},{56,64},{64,7... | collective-permute-start | bytes 884744 | tf_op jit(solution)/shard_map/ppermute | solution.py:13
  9.8 41.3 %collective-permute-start.1 = (bf16[2,1,3,16,1536]{4,3,2,1,0:T(8,128)(2,1)S(1)}, bf16[2,1,3,16,1536]{4,3,2,1,0:T(8,128)(2,1)S(1)}, u32[]{:S(2)}, u32[]{:S(2)}) collective-permute-start(bf16[2,1,3,16,1536]{4,3,2,1,0:T(8,128)(2,1)S(1)} %get-tuple-element.132), channel_id=1, source_target_pairs={{8,0},{16,8},{24,16},{32,24},{40,32},{48,40},{56,48},{64,56},{72,6... | collective-permute-start | bytes 884744 | tf_op jit(solution)/shard_map/ppermute | solution.py:16
  51.3 8.3 %collective-permute-start.2 = (bf16[2,1,10,3,1536]{4,3,2,1,0:T(4,128)(2,1)S(1)}, bf16[2,1,10,3,1536]{4,3,2,1,0:T(4,128)(2,1)S(1)}, u32[]{:S(2)}, u32[]{:S(2)}) collective-permute-start(bf16[2,1,10,3,1536]{4,3,2,1,0:T(4,128)(2,1)S(1)} %get-tuple-element.129), channel_id=1, source_target_pairs={{0,1},{1,2},{2,3},{3,4},{4,5},{5,6},{6,7},{8,9},{9,10},{10,11},{11... | collective-permute-start | bytes 552968 | tf_op jit(solution)/shard_map/ppermute | solution.py:13
  56.0 13.5 %collective-permute-start.3 = (bf16[2,1,10,3,1536]{4,3,2,1,0:T(4,128)(2,1)S(1)}, bf16[2,1,10,3,1536]{4,3,2,1,0:T(4,128)(2,1)S(1)}, u32[]{:S(2)}, u32[]{:S(2)}) collective-permute-start(bf16[2,1,10,3,1536]{4,3,2,1,0:T(4,128)(2,1)S(1)} %get-tuple-element.130), channel_id=1, source_target_pairs={{1,0},{2,1},{3,2},{4,3},{5,4},{6,5},{7,6},{9,8},{10,9},{11,10},{12... | collective-permute-start | bytes 552968 | tf_op jit(solution)/shard_map/ppermute | solution.py:16
Sparse Core Ops, SparseCore 0:
  49.9 67.5 all-gather.2
where the time goes:
time: 316 us; the launch traced here: 313 us
  local copies, waits for them, and re-layouts  129 us (41%)
  other arithmetic  78.6 us (25%)
  blocking collectives  34.5 us (11%)
  loops' own time  28.2 us (9%)
  between operations  13.6 us (4%)
  starting transfers between devices  13.1 us (4%)
  waiting for transfers between devices  11.5 us (4%)
  matrix products  4.55 us (1%)
    convert_element_type x49, local copies, waits for them, and re-layouts, value_step(): window.astype(jnp.float32)  62.9 us
    another operation x49, local copies, waits for them, and re-layouts  42.4 us
    all_gather x1, blocking collectives, shards(): tall_weight = lax.all_gather(out_weight, 'col', axis=0, tiled=True)  34.5 us
    add x7, other arithmetic, value_step(): return (summed + row_total, None)  33.4 us
    dot_general x7, other arithmetic, score_step(): jnp.einsum('ibshd,ibshd->ibsh', query_heads, window, preferred_element_ty...  19.2 us
    another operation x1, loops' own time, shards(): lax.scan(score_step, jnp.zeros((), jnp.float32), row_steps)  14.3 us
    another operation x1, loops' own time, shards(): lax.scan(value_step, initial_sum, (row_steps, attention_grid))  13.9 us
    convert_element_type x7, other arithmetic, value_step(): window.astype(jnp.float32)  10.4 us
  transfers between devices with their start and end apart: 5, of which 2 were waited for; matrix products, arithmetic and copies ran while one was open for 66% of the time, Pallas kernels for 0%

commit v1 on v0

--- a/solution.py
+++ b/solution.py
@@ -86,7 +86,9 @@
     tall_weight = lax.all_gather(out_weight, "col", axis=0, tiled=True)
     result = jnp.dot(
         mixed_heads,
-        lax.all_gather(tall_weight, "row", axis=1, tiled=True),
+        jnp.concatenate(
+            lax.all_to_all(jnp.stack([tall_weight] * lax.axis_size("row")), "row", 0, 0), axis=1
+        ),
         preferred_element_type=jnp.float32,
     )
     return result.astype(jnp.bfloat16).reshape(images, band_rows, strip_cols, model_width)

time: 316 us -> 336 us (1.063)
  the two profiles are of different devices: /device:TPU:248 before, /device:TPU:25 now
where the time goes in v1:
time: 336 us; the launch traced here: 332 us
  local copies, waits for them, and re-layouts  135 us (40%)
  other arithmetic  81.2 us (24%)
  blocking collectives  30.8 us (9%)
  loops' own time  28.1 us (8%)
  starting transfers between devices  27.9 us (8%)
  waiting for transfers between devices  24.5 us (7%)
  matrix products  4.55 us (1%)
    convert_element_type x49, local copies, waits for them, and re-layouts, value_step(): window.astype(jnp.float32)  61.9 us
    another operation x49, local copies, waits for them, and re-layouts  42.4 us
    add x7, other arithmetic, value_step(): return (summed + row_total, None)  33.8 us
    all_gather x1, blocking collectives, shards(): tall_weight = lax.all_gather(out_weight, 'col', axis=0, tiled=True)  30.8 us
    dot_general x7, other arithmetic, score_step(): jnp.einsum('ibshd,ibshd->ibsh', query_heads, window, preferred_element_ty...  19.1 us
    all_to_all x1, starting transfers between devices, shards(): lax.all_to_all(jnp.stack([tall_weight] * lax.axis_size('row')), 'row', 0, 0)  15.3 us
    another operation x1, loops' own time, shards(): lax.scan(score_step, jnp.zeros((), jnp.float32), row_steps)  14.3 us
    ppermute x2, waiting for transfers between devices, extended_2(): lax.ppermute(lax.slice_in_dim(block, block.shape[dim] - width, None, axis...  14.2 us
  transfers between devices with their start and end apart: 5, of which 2 were waited for; matrix products, arithmetic and copies ran while one was open for 65% of the time, Pallas kernels for 0%

profile of v1, /device:TPU:25, one launch (start us, length us, event | category | flops | bytes accessed | tf_op | source)
XLA Modules:
  0.0 331.9 jit_solution(17330656322159591841)
XLA Ops:
  1.2 3.7 %collective-permute-start = (bf16[2,1,3,16,1536]{4,3,2,1,0:T(8,128)(2,1)S(1)}, bf16[2,1,3,16,1536]{4,3,2,1,0:T(8,128)(2,1)S(1)}, u32[]{:S(2)}, u32[]{:S(2)}) collective-permute-start(bf16[2,1,3,16,1536]{4,3,2,1,0:T(8,128)(2,1)S(1)} %get-tuple-element.131), channel_id=1, source_target_pairs={{0,8},{8,16},{16,24},{24,32},{32,40},{40,48},{48,56},{56,64},{64,7... | collective-permute-start | bytes 884744 | tf_op jit(solution)/shard_map/ppermute | solution.py:13
  6.8 30.8 %all-gather = bf16[8,192,48]{1,2,0:T(8,128)(2,1)S(1)} all-gather(bf16[1,192,48]{1,2,0:T(8,128)(2,1)} %bitcast.139), channel_id=1, replica_groups=mesh['row'=32,'col'=8] {'col'}, dimensions={0}, use_global_device_ids=true | all-gather | bytes 165888 | tf_op jit(solution)/shard_map/all_gather | solution.py:86
  37.9 2.7 stack.35
  40.6 15.3 %all-to-all-start = ((bf16[32,1536,48]{1,2,0:T(8,128)(2,1)}), bf16[32,1536,48]{1,2,0:T(8,128)(2,1)}, u32[]{:S(2)}, u32[]{:S(2)}) async-start(bf16[32,1536,48]{1,2,0:T(8,128)(2,1)} %stack.35), calls=%async_computation | async-start | bytes 9437184 | tf_op jit(solution)/shard_map/all_to_all | solution.py:90
  57.4 5.1 %collective-permute-start.2 = (bf16[2,1,10,3,1536]{4,3,2,1,0:T(4,128)(2,1)S(1)}, bf16[2,1,10,3,1536]{4,3,2,1,0:T(4,128)(2,1)S(1)}, u32[]{:S(2)}, u32[]{:S(2)}) collective-permute-start(bf16[2,1,10,3,1536]{4,3,2,1,0:T(4,128)(2,1)S(1)} %get-tuple-element.129), channel_id=1, source_target_pairs={{0,1},{1,2},{2,3},{3,4},{4,5},{5,6},{6,7},{8,9},{9,10},{10,11},{11... | collective-permute-start | bytes 552968 | tf_op jit(solution)/shard_map/ppermute | solution.py:13
  64.6 14.2 %collective-permute-done.2 = bf16[2,1,10,3,1536]{4,3,2,1,0:T(4,128)(2,1)S(1)} collective-permute-done((bf16[2,1,10,3,1536]{4,3,2,1,0:T(4,128)(2,1)S(1)}, bf16[2,1,10,3,1536]{4,3,2,1,0:T(4,128)(2,1)S(1)}, u32[]{:S(2)}, u32[]{:S(2)}) %collective-permute-start.2) | collective-permute-done | bytes 184352 | tf_op jit(solution)/shard_map/ppermute | solution.py:13
  78.8 10.3 %collective-permute-done.3 = bf16[2,1,10,3,1536]{4,3,2,1,0:T(4,128)(2,1)S(1)} collective-permute-done((bf16[2,1,10,3,1536]{4,3,2,1,0:T(4,128)(2,1)S(1)}, bf16[2,1,10,3,1536]{4,3,2,1,0:T(4,128)(2,1)S(1)}, u32[]{:S(2)}, u32[]{:S(2)}) %collective-permute-start.3) | collective-permute-done | bytes 184352 | tf_op jit(solution)/shard_map/ppermute | solution.py:16
  89.9 92.9 %while.21 = (s32[]{:T(128)}, f32[7,7,1,4,16,24]{5,4,3,2,1,0:T(8,128)}, s32[7]{0:T(128)S(1)}, bf16[1,10,22,1536]{3,2,1,0:T(8,128)(2,1)S(1)}, bf16[1,4,16,24,64]{4...) while((s32[]{:T(128)}, ...), condition=%wide.region_1.2_spmd, body=%wide.region_0.1_spmd.sunk | while | flops 2151947 | bytes 7825699 | solution.py:64
  99.6 2.7 fusion.23
  112.9 2.7 fusion.23
  126.2 2.7 fusion.23
  139.4 2.7 fusion.23
  152.7 2.7 fusion.23
  166.0 2.7 fusion.23
  179.2 2.7 fusion.23
  187.4 138.6 %while.22 = (s32[]{:T(128)}, f32[1,4,16,24,64]{4,3,2,1,0:T(8,128)}, bf16[7,7,1,4,16,24]{5,4,3,2,1,0:T(8,128)(2,1)}, s32[7]{0:T(128)}, bf16[1,10,22,1536]{3,2,1,0...) while((s32[]{:T(128)}, f32[1,4,16,24,64]{4,3,2,1,0:T(8,128)}, ...), condition=%wide.region_5.6_spmd.clone, body=%wide.region_4.5_spmd.clone.sunk | while | flops 2173452 | bytes 13280581 | solution.py:84
  202.3 4.7 %select_add_fusion.2 = f32[1,4,16,24,64]{4,3,2,1,0:T(8,128)} fusion(f32[1,4,16,24,64]{4,3,2,1,0:T(8,128)} %get-tuple-element.308, f32[1,4,16,24,64]{4,3,2,1,0:T(8,128)S(1)} %reshape.523, f32[1,4,16,24,64]{4,3,2,1,0:T(8,128)S(1)} %reshape.524, f32[1,4,16,24,64]{4,3,2,1,0:T(8,128)S(1)} %reshape.525, f32[1,4,16,24,64]{4,3,2,1,0:T(8,128)} %reshape.526, ...), kind=kLoop, calls=%fused_computation.clone.1 | loop fusion | flops 1474560 | bytes 3581953 | tf_op jit(solution)/shard_map/while/body/eval_jaxpr/add | solution.py:81
  222.0 4.8 %select_add_fusion.2 = f32[1,4,16,24,64]{4,3,2,1,0:T(8,128)} fusion(f32[1,4,16,24,64]{4,3,2,1,0:T(8,128)} %get-tuple-element.308, f32[1,4,16,24,64]{4,3,2,1,0:T(8,128)S(1)} %reshape.523, f32[1,4,16,24,64]{4,3,2,1,0:T(8,128)S(1)} %reshape.524, f32[1,4,16,24,64]{4,3,2,1,0:T(8,128)S(1)} %reshape.525, f32[1,4,16,24,64]{4,3,2,1,0:T(8,128)} %reshape.526, ...), kind=kLoop, calls=%fused_computation.clone.1 | loop fusion | flops 1474560 | bytes 3581953 | tf_op jit(solution)/shard_map/while/body/eval_jaxpr/add | solution.py:81
  241.8 4.8 %select_add_fusion.2 = f32[1,4,16,24,64]{4,3,2,1,0:T(8,128)} fusion(f32[1,4,16,24,64]{4,3,2,1,0:T(8,128)} %get-tuple-element.308, f32[1,4,16,24,64]{4,3,2,1,0:T(8,128)S(1)} %reshape.523, f32[1,4,16,24,64]{4,3,2,1,0:T(8,128)S(1)} %reshape.524, f32[1,4,16,24,64]{4,3,2,1,0:T(8,128)S(1)} %reshape.525, f32[1,4,16,24,64]{4,3,2,1,0:T(8,128)} %reshape.526, ...), kind=kLoop, calls=%fused_computation.clone.1 | loop fusion | flops 1474560 | bytes 3581953 | tf_op jit(solution)/shard_map/while/body/eval_jaxpr/add | solution.py:81
  261.6 4.8 %select_add_fusion.2 = f32[1,4,16,24,64]{4,3,2,1,0:T(8,128)} fusion(f32[1,4,16,24,64]{4,3,2,1,0:T(8,128)} %get-tuple-element.308, f32[1,4,16,24,64]{4,3,2,1,0:T(8,128)S(1)} %reshape.523, f32[1,4,16,24,64]{4,3,2,1,0:T(8,128)S(1)} %reshape.524, f32[1,4,16,24,64]{4,3,2,1,0:T(8,128)S(1)} %reshape.525, f32[1,4,16,24,64]{4,3,2,1,0:T(8,128)} %reshape.526, ...), kind=kLoop, calls=%fused_computation.clone.1 | loop fusion | flops 1474560 | bytes 3581953 | tf_op jit(solution)/shard_map/while/body/eval_jaxpr/add | solution.py:81
  281.4 4.8 %select_add_fusion.2 = f32[1,4,16,24,64]{4,3,2,1,0:T(8,128)} fusion(f32[1,4,16,24,64]{4,3,2,1,0:T(8,128)} %get-tuple-element.308, f32[1,4,16,24,64]{4,3,2,1,0:T(8,128)S(1)} %reshape.523, f32[1,4,16,24,64]{4,3,2,1,0:T(8,128)S(1)} %reshape.524, f32[1,4,16,24,64]{4,3,2,1,0:T(8,128)S(1)} %reshape.525, f32[1,4,16,24,64]{4,3,2,1,0:T(8,128)} %reshape.526, ...), kind=kLoop, calls=%fused_computation.clone.1 | loop fusion | flops 1474560 | bytes 3581953 | tf_op jit(solution)/shard_map/while/body/eval_jaxpr/add | solution.py:81
  301.2 4.8 %select_add_fusion.2 = f32[1,4,16,24,64]{4,3,2,1,0:T(8,128)} fusion(f32[1,4,16,24,64]{4,3,2,1,0:T(8,128)} %get-tuple-element.308, f32[1,4,16,24,64]{4,3,2,1,0:T(8,128)S(1)} %reshape.523, f32[1,4,16,24,64]{4,3,2,1,0:T(8,128)S(1)} %reshape.524, f32[1,4,16,24,64]{4,3,2,1,0:T(8,128)S(1)} %reshape.525, f32[1,4,16,24,64]{4,3,2,1,0:T(8,128)} %reshape.526, ...), kind=kLoop, calls=%fused_computation.clone.1 | loop fusion | flops 1474560 | bytes 3581953 | tf_op jit(solution)/shard_map/while/body/eval_jaxpr/add | solution.py:81
  321.1 4.8 %select_add_fusion.2 = f32[1,4,16,24,64]{4,3,2,1,0:T(8,128)} fusion(f32[1,4,16,24,64]{4,3,2,1,0:T(8,128)} %get-tuple-element.308, f32[1,4,16,24,64]{4,3,2,1,0:T(8,128)S(1)} %reshape.523, f32[1,4,16,24,64]{4,3,2,1,0:T(8,128)S(1)} %reshape.524, f32[1,4,16,24,64]{4,3,2,1,0:T(8,128)S(1)} %reshape.525, f32[1,4,16,24,64]{4,3,2,1,0:T(8,128)} %reshape.526, ...), kind=kLoop, calls=%fused_computation.clone.1 | loop fusion | flops 1474560 | bytes 3581953 | tf_op jit(solution)/shard_map/while/body/eval_jaxpr/add | solution.py:81
  327.4 4.5 %convolution_convert_fusion = bf16[64,1536]{1,0:T(8,128)(2,1)} fusion(bf16[64,1536]{1,0:T(8,128)(2,1)S(1)} %reshape.447, bf16[1536,1536]{0,1:T(8,128)(2,1)} %bitcast.17), kind=kOutput, calls=%fused_computation.51 | convolution fusion | flops 302088192 | bytes 5111808 | tf_op jit(solution)/shard_map/dot_general | solution.py:87
  (228 shorter events, 164.0 us)
Async XLA Ops:
  1.2 56.0 %collective-permute-start = (bf16[2,1,3,16,1536]{4,3,2,1,0:T(8,128)(2,1)S(1)}, bf16[2,1,3,16,1536]{4,3,2,1,0:T(8,128)(2,1)S(1)}, u32[]{:S(2)}, u32[]{:S(2)}) collective-permute-start(bf16[2,1,3,16,1536]{4,3,2,1,0:T(8,128)(2,1)S(1)} %get-tuple-element.131), channel_id=1, source_target_pairs={{0,8},{8,16},{16,24},{24,32},{32,40},{40,48},{48,56},{56,64},{64,7... | collective-permute-start | bytes 884744 | tf_op jit(solution)/shard_map/ppermute | solution.py:13
  4.9 52.3 %collective-permute-start.1 = (bf16[2,1,3,16,1536]{4,3,2,1,0:T(8,128)(2,1)S(1)}, bf16[2,1,3,16,1536]{4,3,2,1,0:T(8,128)(2,1)S(1)}, u32[]{:S(2)}, u32[]{:S(2)}) collective-permute-start(bf16[2,1,3,16,1536]{4,3,2,1,0:T(8,128)(2,1)S(1)} %get-tuple-element.132), channel_id=1, source_target_pairs={{8,0},{16,8},{24,16},{32,24},{40,32},{48,40},{56,48},{64,56},{72,6... | collective-permute-start | bytes 884744 | tf_op jit(solution)/shard_map/ppermute | solution.py:16
  40.6 15.3 %copy-start.4 = (f32[24,49]{1,0:T(8,128)S(1)}, f32[24,49]{1,0:T(8,128)}, u32[]{:S(2)}) copy-start(f32[24,49]{1,0:T(8,128)} %param.12) | copy-start | bytes 14116
  40.6 15.4 %copy-start.3 = (bf16[1,4,16,1536]{3,2,1,0:T(8,128)(2,1)S(1)}, bf16[1,4,16,1536]{3,2,1,0:T(8,128)(2,1)}, u32[]{:S(2)}) copy-start(bf16[1,4,16,1536]{3,2,1,0:T(8,128)(2,1)} %param.9) | copy-start | bytes 589828
  40.6 16.6 %copy-start.1 = (bf16[1,4,16,1536]{3,2,1,0:T(8,128)(2,1)S(1)}, bf16[1,4,16,1536]{3,2,1,0:T(8,128)(2,1)}, u32[]{:S(2)}) copy-start(bf16[1,4,16,1536]{3,2,1,0:T(8,128)(2,1)} %param.10) | copy-start | bytes 589828
  40.6 16.6 %copy-start.2 = (bf16[1,4,16,1536]{3,2,1,0:T(8,128)(2,1)S(1)}, bf16[1,4,16,1536]{3,2,1,0:T(8,128)(2,1)}, u32[]{:S(2)}) copy-start(bf16[1,4,16,1536]{3,2,1,0:T(8,128)(2,1)} %param.11) | copy-start | bytes 589828
  40.6 286.8 %all-to-all-start = ((bf16[32,1536,48]{1,2,0:T(8,128)(2,1)}), bf16[32,1536,48]{1,2,0:T(8,128)(2,1)}, u32[]{:S(2)}, u32[]{:S(2)}) async-start(bf16[32,1536,48]{1,2,0:T(8,128)(2,1)} %stack.35), calls=%async_computation | async-start | bytes 9437184 | tf_op jit(solution)/shard_map/all_to_all | solution.py:90
  57.4 21.4 %collective-permute-start.2 = (bf16[2,1,10,3,1536]{4,3,2,1,0:T(4,128)(2,1)S(1)}, bf16[2,1,10,3,1536]{4,3,2,1,0:T(4,128)(2,1)S(1)}, u32[]{:S(2)}, u32[]{:S(2)}) collective-permute-start(bf16[2,1,10,3,1536]{4,3,2,1,0:T(4,128)(2,1)S(1)} %get-tuple-element.129), channel_id=1, source_target_pairs={{0,1},{1,2},{2,3},{3,4},{4,5},{5,6},{6,7},{8,9},{9,10},{10,11},{11... | collective-permute-start | bytes 552968 | tf_op jit(solution)/shard_map/ppermute | solution.py:13
  62.5 26.5 %collective-permute-start.3 = (bf16[2,1,10,3,1536]{4,3,2,1,0:T(4,128)(2,1)S(1)}, bf16[2,1,10,3,1536]{4,3,2,1,0:T(4,128)(2,1)S(1)}, u32[]{:S(2)}, u32[]{:S(2)}) collective-permute-start(bf16[2,1,10,3,1536]{4,3,2,1,0:T(4,128)(2,1)S(1)} %get-tuple-element.130), channel_id=1, source_target_pairs={{1,0},{2,1},{3,2},{4,3},{5,4},{6,5},{7,6},{9,8},{10,9},{11,10},{12... | collective-permute-start | bytes 552968 | tf_op jit(solution)/shard_map/ppermute | solution.py:16
  182.8 1.9 copy-start
